TPU v7x, 32 devices: a whole 2x2x4 slice. The times are simulated.
32 devices in a mesh: rows: 8 (over y, x, core), feat: 4 (over z).
Axes of the slice: x: 2, y: 2, z: 4, core: 2. Of those that a mesh axis runs over, the one named last changes fastest.
Arguments:
- features: bfloat16 [2048, 512], P('rows', 'feat'), may hold values from -6 to 6
- weight: bfloat16 [512, 512], P(None, 'feat'), may hold values from -0.25 to 0.25
- block_values: bfloat16 [16, 8, 128, 128], P('rows', 'feat'), may hold values from -0.25 to 0.25
- columns: int32 [16, 8], P('rows'), may hold values from 0 to 15, as said below
- counts: int32 [16], P('rows'), may hold values from 2 to 8, as said below
- cotangent: bfloat16 [2048, 512], P('rows', 'feat'), may hold values from -6 to 6
Outputs:
- hidden: bfloat16 [2048, 512], P('rows', 'feat')
- grad_features: bfloat16 [2048, 512], P('rows', 'feat')
- grad_weight: float32 [512, 512], P(None, 'feat')
Inputs may be any that keep to these rules, and one draw needn't show every extreme that they name: `columns`: the 8 column blocks of a row block are distinct and lie on the devices within 2 indices of the row block's own index along rows, counted around the axis (the device of block c is c // 2). Slots 0 to counts[g] - 1 of row block g are live, the others are ignored; some row block has exactly 8 live slots.
All inputs are finite; a program needn't handle non-finite values.
Results may differ from a plain program's by a relative error of at most 0.0067.
Values may be sent and summed in bfloat16 or wider, within the bound.
A program may use at most 64 MiB of HBM per device.

v0:
```python
import jax
import jax.numpy as jnp
from jax import lax
from jax.sharding import PartitionSpec as P


def shifted(value, axis, steps):
    count = lax.axis_size(axis)
    pairs = [(source, (source + steps) % count) for source in range(count)]
    return lax.ppermute(value, axis, pairs)


def activation(values):
    return jax.nn.gelu(values, approximate=True)


def window_index(columns, row_blocks, center, halo_reach, row_count):
    owner_dev = columns // row_blocks
    offset = (owner_dev - center + halo_reach + row_count) % row_count
    return offset * row_blocks + columns % row_blocks


def live_tiles(panel_part, first_slot, counts, places):
    slot_count = panel_part.shape[1]
    slot_ids = first_slot + jnp.arange(slot_count)
    slot_live = counts[:, None] > slot_ids[None, :]
    tiles = jnp.where(slot_live[:, :, None, None], panel_part, jnp.zeros((), panel_part.dtype))
    return (tiles, places)


def gather_slots(panel_part, first_slot, counts, places, window):
    tiles, targets = live_tiles(panel_part, first_slot, counts, places)
    picked = jnp.take(window, targets, axis=0)
    product = jnp.einsum("gsij,gsjf->gif", tiles, picked, preferred_element_type=jnp.float32)
    return product


def spread_slots(running, panel_part, first_slot, counts, places, grad_blocks):
    tiles, targets = live_tiles(panel_part, first_slot, counts, places)
    block_size = grad_blocks.shape[1]
    feat_width = grad_blocks.shape[2]
    product = jnp.einsum("gsij,gif->gsjf", tiles, grad_blocks, preferred_element_type=jnp.float32)
    return running.at[targets.reshape(-1)].add(product.reshape(-1, block_size, feat_width))


def on_device(features, weight, block_values, columns, counts, cotangent):
    row_count = lax.axis_size("rows")
    center = lax.axis_index("rows")
    halo_reach = min(4, (row_count - 1) // 3)
    row_blocks = counts.shape[0]
    block_size = block_values.shape[2]
    feat_width = features.shape[1]
    local_rows = features.shape[0]
    span_blocks = (2 * halo_reach + 1) * row_blocks
    pieces = {0: features}
    for heading in (1, -1):
        current = features
        for distance in range(1, halo_reach + 1):
            current = shifted(current, "rows", -heading)
            pieces[heading * distance] = current
    window = jnp.stack([pieces[offset] for offset in range(-halo_reach, halo_reach + 1)])
    window = window.reshape(span_blocks, block_size, feat_width)
    places = window_index(columns, row_blocks, center, halo_reach, row_count)
    panel_full = lax.all_gather(block_values, "feat", axis=1, tiled=True)
    summed = gather_slots(panel_full, 0, counts, places, window)
    aggregated = summed.reshape(local_rows, feat_width).astype(jnp.bfloat16)
    agg_full, weight_full = (
        lax.all_gather(aggregated, "feat", axis=1, tiled=True),
        lax.all_gather(weight, "feat", axis=1, tiled=True),
    )
    pre_act = jnp.dot(agg_full, weight, preferred_element_type=jnp.float32)
    hidden, act_grad = jax.vjp(activation, pre_act)
    grad_pre = act_grad(cotangent.astype(jnp.float32))[0].astype(jnp.bfloat16)
    grad_full = lax.all_gather(grad_pre, "feat", axis=1, tiled=True)
    weight_terms = lax.dot_general(
        agg_full, grad_pre, (((0,), (0,)), ((), ())), preferred_element_type=jnp.float32
    )
    node_total = local_rows * row_count
    grad_weight = lax.psum(weight_terms, "rows") * float(node_total) ** (-0.5)
    feat_index = lax.axis_index("feat")
    weight_rows = lax.dynamic_slice_in_dim(weight_full, feat_index * feat_width, feat_width, 0)
    grad_agg = lax.dot_general(
        grad_full, weight_rows, (((1,), (1,)), ((), ())), preferred_element_type=jnp.float32
    )
    grad_blocks = grad_agg.astype(jnp.bfloat16).reshape(row_blocks, block_size, feat_width)
    zero_window = jnp.zeros((span_blocks, block_size, feat_width), jnp.float32)
    spread = spread_slots(zero_window, panel_full, 0, counts, places, grad_blocks)
    spread = spread.reshape(2 * halo_reach + 1, local_rows, feat_width)
    grad_local = spread[halo_reach]
    for heading in (1, -1):
        bundle = None
        for distance in range(halo_reach, 0, -1):
            own_piece = spread[halo_reach + heading * distance].astype(jnp.bfloat16)[None]
            if bundle is None:
                outgoing = own_piece
            else:
                outgoing = jnp.concatenate([bundle, own_piece], axis=0)
            bundle = shifted(outgoing, "rows", heading)
        grad_local = grad_local + jnp.sum(bundle.astype(jnp.float32), axis=0)
    return (hidden.astype(jnp.bfloat16), grad_local.astype(jnp.bfloat16), grad_weight)


def solution(mesh):
    in_specs = (
        P("rows", "feat"),
        P(None, "feat"),
        P("rows", "feat", None, None),
        P("rows", None),
        P("rows"),
        P("rows", "feat"),
    )
    out_specs = (P("rows", "feat"), P("rows", "feat"), P(None, "feat"))
    return jax.shard_map(
        on_device, mesh=mesh, in_specs=in_specs, out_specs=out_specs, check_vma=False
    )
```

profile of v0, /device:TPU:0, one launch (start us, length us, event | category | flops | bytes accessed | tf_op | source)
XLA Modules:
  0.0 141.4 jit_solution(15780975952364589726)
XLA Ops:
  7.2 0.0 all-reduce.2.cloned.1.call-start
  7.2 0.5 collective-permute-start
  7.7 2.9 %collective-permute-start.2 = (bf16[256,128]{1,0:T(8,128)(2,1)}, bf16[256,128]{1,0:T(8,128)(2,1)S(1)}, u32[]{:S(2)}, u32[]{:S(2)}) collective-permute-start(bf16[256,128]{1,0:T(8,128)(2,1)} %param.6), channel_id=1, source_target_pairs={{0,28},{4,0},{8,4},{12,8},{16,12},{20,16},{24,20},{28,24},{1,29},{... | collective-permute-start | bytes 196616 | tf_op jit(solution)/shard_map/ppermute | solution.py:10
  10.7 0.7 copy-done.2
  11.4 0.1 reshape.130
  11.5 0.6 copy-done.4
  12.1 0.1 iota_compare_fusion
  12.2 16.2 %all_gather.12 = bf16[2,8,128,128]{3,2,1,0:T(8,128)(2,1)S(1)} all-gather(bf16[2,2,128,128]{3,2,1,0:T(8,128)(2,1)} %param.8), channel_id=1, replica_groups=mesh['rows'=8,'feat'=4] {'feat'}, dimensions={1}, use_global_device_ids=true | all-gather | bytes 655360 | tf_op jit(solution)/shard_map/all_gather | solution.py:64
  28.4 15.0 %all_gather.15 = bf16[512,512]{1,0:T(8,128)(2,1)S(1)} all-gather(bf16[512,128]{1,0:T(8,128)(2,1)S(1)} %copy-done), channel_id=1, replica_groups=mesh['rows'=8,'feat'=4] {'feat'}, dimensions={1}, use_global_device_ids=true | all-gather | bytes 655360 | tf_op jit(solution)/shard_map/all_gather | solution.py:69
  43.4 0.1 reshape.135
  43.5 2.7 %collective-permute-start.3 = (bf16[256,128]{1,0:T(8,128)(2,1)S(1)}, bf16[256,128]{1,0:T(8,128)(2,1)S(1)}, u32[]{:S(2)}, u32[]{:S(2)}) collective-permute-start(bf16[256,128]{1,0:T(8,128)(2,1)S(1)} %collective-permute-done.2), channel_id=1, source_target_pairs={{0,28},{4,0},{8,4},{12,8},{16,12},{20,16},{24,20},{28,24},{1,29},{... | collective-permute-start | bytes 196616 | tf_op jit(solution)/shard_map/ppermute | solution.py:10
  46.2 1.9 %collective-permute-done.1 = bf16[256,128]{1,0:T(8,128)(2,1)S(1)} collective-permute-done((bf16[256,128]{1,0:T(8,128)(2,1)S(1)}, bf16[256,128]{1,0:T(8,128)(2,1)S(1)}, u32[]{:S(2)}, u32[]{:S(2)}) %collective-permute-start.1) | collective-permute-done | bytes 65568 | tf_op jit(solution)/shard_map/ppermute | solution.py:10
  48.1 0.8 copy-done.1
  49.0 0.6 gather_fusion
  49.6 0.4 fusion
  50.0 12.9 %all_gather.13 = bf16[256,512]{1,0:T(8,128)(2,1)S(1)} all-gather(bf16[256,128]{1,0:T(8,128)(2,1)S(1)} %bitcast.48), channel_id=1, replica_groups=mesh['rows'=8,'feat'=4] {'feat'}, dimensions={1}, use_global_device_ids=true | all-gather | bytes 327680 | tf_op jit(solution)/shard_map/all_gather | solution.py:68
  62.9 0.9 fusion.9
  63.8 12.8 %all_gather.14 = bf16[256,512]{1,0:T(8,128)(2,1)S(1)} all-gather(bf16[256,128]{1,0:T(8,128)(2,1)S(1)} %get-tuple-element.9), channel_id=1, replica_groups=mesh['rows'=8,'feat'=4] {'feat'}, dimensions={1}, use_global_device_ids=true | all-gather | bytes 327680 | tf_op jit(solution)/shard_map/all_gather | solution.py:74
  76.6 0.2 convolution_convert_fusion
  76.8 0.4 fusion.3
  77.3 1.6 %scatter_fusion = f32[10,128,128]{2,1,0:T(8,128)S(1)} fusion(f32[10,128,128]{2,1,0:T(8,128)S(1)} %broadcast_in_dim.47, s32[16]{0:T(128)S(1)} %fusion.23, f32[16,128,128]{2,1,0:T(8,128)S(1)} %bitcast.42), kind=kCustom, calls=%fused_computation.1 | custom fusion | flops 262144 | bytes 3145792 | tf_op jit(solution)/shard_map/scatter-add | solution.py:43
  78.9 0.1 convert.6
  79.0 0.1 collective-permute-start.6
  79.1 1.0 fusion.30
  80.1 0.5 collective-permute-start.4
  80.6 0.3 collective-permute-done.6
  81.0 2.7 %collective-permute-start.7 = (bf16[2,256,128]{2,1,0:T(8,128)(2,1)S(1)}, bf16[2,256,128]{2,1,0:T(8,128)(2,1)S(1)}, u32[]{:S(2)}, u32[]{:S(2)}) collective-permute-start(bf16[2,256,128]{2,1,0:T(8,128)(2,1)S(1)} %pad_maximum_fusion.1), channel_id=1, source_target_pairs={{0,28},{4,0},{8,4},{12,8},{16,12},{20,16},{24,20},{28,24},{1,29},{... | collective-permute-start | bytes 393224 | tf_op jit(solution)/shard_map/ppermute | solution.py:10
  83.7 1.0 collective-permute-done.4
  84.7 0.1 collective-permute-start.5
  84.8 47.4 %all-reduce.2.cloned.1.call-done = f32[512,128]{1,0:T(8,128)} async-done(((f32[512,128]{1,0:T(8,128)}), f32[512,128]{1,0:T(8,128)}) %all-reduce.2.cloned.1.call-update) | async-done | bytes 262160 | tf_op jit(solution)/shard_map/psum | solution.py:79
  132.2 1.7 %broadcast_multiply_fusion = f32[512,128]{1,0:T(8,128)} fusion(f32[512,128]{1,0:T(8,128)} %all-reduce.2.cloned.1.call-done), kind=kLoop, calls=%fused_computation.33 | loop fusion | flops 65536 | bytes 524288 | tf_op jit(solution)/shard_map/mul | solution.py:79
  133.9 0.7 fusion.18
  (30 shorter events, 0.3 us)
Async XLA Ops:
  7.2 125.0 %all-reduce.2.cloned.1.call-start = ((), (), s32[]{:S(2)}) async-start(), calls=%async_computation | async-start | bytes 524288 | tf_op jit(solution)/shard_map/psum | solution.py:79
  7.2 36.3 %collective-permute-start = (bf16[256,128]{1,0:T(8,128)(2,1)}, bf16[256,128]{1,0:T(8,128)(2,1)S(1)}, u32[]{:S(2)}, u32[]{:S(2)}) collective-permute-start(bf16[256,128]{1,0:T(8,128)(2,1)} %param.6), channel_id=1, source_target_pairs={{0,4},{4,8},{8,12},{12,16},{16,20},{20,24},{24,28},{28,0},{1,5},{5... | collective-permute-start | bytes 196616 | tf_op jit(solution)/shard_map/ppermute | solution.py:10
  7.7 35.8 %collective-permute-start.2 = (bf16[256,128]{1,0:T(8,128)(2,1)}, bf16[256,128]{1,0:T(8,128)(2,1)S(1)}, u32[]{:S(2)}, u32[]{:S(2)}) collective-permute-start(bf16[256,128]{1,0:T(8,128)(2,1)} %param.6), channel_id=1, source_target_pairs={{0,28},{4,0},{8,4},{12,8},{16,12},{20,16},{24,20},{28,24},{1,29},{... | collective-permute-start | bytes 196616 | tf_op jit(solution)/shard_map/ppermute | solution.py:10
  10.7 0.7 copy-start.2
  11.5 0.7 copy-start.4
  12.2 16.2 %copy-start = (bf16[512,128]{1,0:T(8,128)(2,1)S(1)}, bf16[512,128]{1,0:T(8,128)(2,1)}, u32[]{:S(2)}) copy-start(bf16[512,128]{1,0:T(8,128)(2,1)} %param.7) | copy-start | bytes 393220
  43.5 4.6 %collective-permute-start.1 = (bf16[256,128]{1,0:T(8,128)(2,1)S(1)}, bf16[256,128]{1,0:T(8,128)(2,1)S(1)}, u32[]{:S(2)}, u32[]{:S(2)}) collective-permute-start(bf16[256,128]{1,0:T(8,128)(2,1)S(1)} %collective-permute-done), channel_id=1, source_target_pairs={{0,4},{4,8},{8,12},{12,16},{16,20},{20,24},{24,28},{28,0},{1,5},{5... | collective-permute-start | bytes 196616 | tf_op jit(solution)/shard_map/ppermute | solution.py:10
  43.5 5.4 %collective-permute-start.3 = (bf16[256,128]{1,0:T(8,128)(2,1)S(1)}, bf16[256,128]{1,0:T(8,128)(2,1)S(1)}, u32[]{:S(2)}, u32[]{:S(2)}) collective-permute-start(bf16[256,128]{1,0:T(8,128)(2,1)S(1)} %collective-permute-done.2), channel_id=1, source_target_pairs={{0,28},{4,0},{8,4},{12,8},{16,12},{20,16},{24,20},{28,24},{1,29},{... | collective-permute-start | bytes 196616 | tf_op jit(solution)/shard_map/ppermute | solution.py:10
  48.1 0.8 copy-start.1
  50.0 12.9 %copy-start.3 = (bf16[256,128]{1,0:T(8,128)(2,1)S(1)}, bf16[256,128]{1,0:T(8,128)(2,1)}, u32[]{:S(2)}) copy-start(bf16[256,128]{1,0:T(8,128)(2,1)} %param.11) | copy-start | bytes 196612
  79.0 2.0 %collective-permute-start.6 = (bf16[1,256,128]{2,1,0:T(8,128)(2,1)S(1)}, bf16[1,256,128]{2,1,0:T(8,128)(2,1)S(1)}, u32[]{:S(2)}, u32[]{:S(2)}) collective-permute-start(bf16[1,256,128]{2,1,0:T(8,128)(2,1)S(1)} %bitcast.50), channel_id=1, source_target_pairs={{0,28},{4,0},{8,4},{12,8},{16,12},{20,16},{24,20},{28,24},{1,29},{... | collective-permute-start | bytes 196616 | tf_op jit(solution)/shard_map/ppermute | solution.py:10
  80.1 4.6 %collective-permute-start.4 = (bf16[1,256,128]{2,1,0:T(8,128)(2,1)S(1)}, bf16[1,256,128]{2,1,0:T(8,128)(2,1)S(1)}, u32[]{:S(2)}, u32[]{:S(2)}) collective-permute-start(bf16[1,256,128]{2,1,0:T(8,128)(2,1)S(1)} %bitcast.49), channel_id=1, source_target_pairs={{0,4},{4,8},{8,12},{12,16},{16,20},{20,24},{24,28},{28,0},{1,5},{5... | collective-permute-start | bytes 196616 | tf_op jit(solution)/shard_map/ppermute | solution.py:10
  81.0 52.9 %collective-permute-start.7 = (bf16[2,256,128]{2,1,0:T(8,128)(2,1)S(1)}, bf16[2,256,128]{2,1,0:T(8,128)(2,1)S(1)}, u32[]{:S(2)}, u32[]{:S(2)}) collective-permute-start(bf16[2,256,128]{2,1,0:T(8,128)(2,1)S(1)} %pad_maximum_fusion.1), channel_id=1, source_target_pairs={{0,28},{4,0},{8,4},{12,8},{16,12},{20,16},{24,20},{28,24},{1,29},{... | collective-permute-start | bytes 393224 | tf_op jit(solution)/shard_map/ppermute | solution.py:10
  84.7 49.1 %collective-permute-start.5 = (bf16[2,256,128]{2,1,0:T(8,128)(2,1)S(1)}, bf16[2,256,128]{2,1,0:T(8,128)(2,1)S(1)}, u32[]{:S(2)}, u32[]{:S(2)}) collective-permute-start(bf16[2,256,128]{2,1,0:T(8,128)(2,1)S(1)} %pad_maximum_fusion), channel_id=1, source_target_pairs={{0,4},{4,8},{8,12},{12,16},{16,20},{20,24},{24,28},{28,0},{1,5},{5... | collective-permute-start | bytes 393224 | tf_op jit(solution)/shard_map/ppermute | solution.py:10
Sparse Core Ops, SparseCore 0:
  80.2 51.9 all-reduce.1
where the time goes:
time: 142 us; the launch traced here: 141 us
  blocking collectives  56.9 us (40%)
  waiting for transfers between devices  50.6 us (36%)
  between operations  14.2 us (10%)
  starting transfers between devices  9.58 us (7%)
  other arithmetic  4.16 us (3%)
  local copies, waits for them, and re-layouts  3.1 us (2%)
  matrix products  2.89 us (2%)
    psum x1, waiting for transfers between devices, on_device(): grad_weight = lax.psum(weight_terms, 'rows') * float(node_total) ** (-0.5)  47.4 us
    all_gather x1, blocking collectives, on_device(): panel_full = lax.all_gather(block_values, 'feat', axis=1, tiled=True)  16.2 us
    all_gather x1, blocking collectives, on_device(): lax.all_gather(weight, 'feat', axis=1, tiled=True)  15 us
    all_gather x1, blocking collectives, on_device(): lax.all_gather(aggregated, 'feat', axis=1, tiled=True)  12.9 us
    all_gather x1, blocking collectives, on_device(): grad_full = lax.all_gather(grad_pre, 'feat', axis=1, tiled=True)  12.8 us
    ppermute x8, starting transfers between devices, shifted(): return lax.ppermute(value, axis, pairs)  9.54 us
    ppermute x8, waiting for transfers between devices, shifted(): return lax.ppermute(value, axis, pairs)  3.23 us
  transfers between devices with their start and end apart: 9, of which 4 were waited for; matrix products, arithmetic and copies ran while one was open for 2% of the time, Pallas kernels for 0%

commit v1 on v0

v1 whole, which is shorter than its diff:
```python
import functools

import jax
import jax.numpy as jnp
from jax import lax
from jax.experimental import pallas as pl
from jax.experimental.pallas import tpu as pltpu
from jax.sharding import PartitionSpec as P

MESH = pl.DeviceIdType.MESH
F32 = jnp.float32
BF16 = jnp.bfloat16
GELU_SCALE = 0.7978845608028654
GELU_CUBE = 0.044715


def gelu_and_slope(v):
    square = v * v
    t = jnp.tanh(GELU_SCALE * (v + GELU_CUBE * (square * v)))
    half = 0.5 * (1.0 + t)
    inner = GELU_SCALE * (1.0 + 3.0 * GELU_CUBE * square)
    return v * half, half + 0.5 * v * (1.0 - t * t) * inner


def dot(a, b, contract):
    return lax.dot_general(a, b, (contract, ((), ())), preferred_element_type=F32)


def kernel(n, m, reach, rb, sl, in_sum, cols, cnt, x_ref, w_ref, t_ref, ct_ref,
           hid_ref, gf_ref, gw_ref, xall, wrow, tl, yw, sw, sr, gall, gpart, gwp, gwr, gwa,
           send_sem, recv_sem):
    r = lax.axis_index("rows")
    f = lax.axis_index("feat")
    fb = t_ref.shape[1]
    rows = rb * fb
    fw = x_ref.shape[1]
    per = rb * sl
    chunk = gwr.shape[1]
    halo = [o for d in range(1, reach + 1) for o in (d, -d)]
    feat_d = list(range(1, m))
    row_d = list(range(1, n)) if in_sum else []
    row_peers = [d % n for d in (row_d if in_sum else halo)]

    barrier = pltpu.get_barrier_semaphore()
    for d in feat_d:
        pl.semaphore_signal(barrier, inc=1, device_id={"feat": lax.rem(f + d, m)}, device_id_type=MESH)
    for d in row_peers:
        pl.semaphore_signal(barrier, inc=1, device_id={"rows": lax.rem(r + d, n)}, device_id_type=MESH)
    pl.semaphore_wait(barrier, len(feat_d) + len(row_peers))

    started = []

    def push(src, dst, axis, peer):
        at = len(started)
        copy = pltpu.make_async_remote_copy(
            src_ref=src, dst_ref=dst, send_sem=send_sem.at[at], recv_sem=recv_sem.at[at],
            device_id={axis: peer}, device_id_type=MESH)
        copy.start()
        started.append(copy)
        return copy

    x_in = {d: push(x_ref, xall.at[d], "feat", lax.rem(f + d, m)) for d in feat_d}
    t_in = {d: push(t_ref, tl.at[pl.ds(d * per, per)], "feat", lax.rem(f + d, m)) for d in feat_d}
    w_in = {}
    for d in feat_d:
        peer = lax.rem(f + d, m)
        w_in[d] = push(w_ref.at[pl.ds(pl.multiple_of(peer * fw, fw), fw)], wrow.at[d], "feat", peer)

    source = [lax.rem(f + m - d, m) for d in range(m)]

    def weight_rows(d):
        return w_ref[pl.ds(pl.multiple_of(source[d] * fw, fw), fw), :]

    zero_tile = m * per
    place = {}
    for d in range(m):
        for g in range(rb):
            for j in range(sl):
                s = source[d] * sl + j
                col = cols[g, s]
                offset = lax.rem(lax.div(col, rb) - r + reach + n, n)
                live = cnt[g] > s
                at = (d * rb + g) * sl + j
                place[at] = (g, live, offset * rb + lax.rem(col, rb))
    inverse = {}
    for c in range((2 * reach + 1) * rb):
        for g in range(rb):
            found = jnp.int32(zero_tile)
            for at, (group, live, where) in place.items():
                if group == g:
                    found = jnp.where(jnp.logical_and(live, where == c), at, found)
            inverse[c, g] = found

    tl[pl.ds(0, per)] = t_ref[...]
    tl[zero_tile] = jnp.zeros((fb, fb), BF16)

    order = [d for pair in zip(range(1, m), range(m - 1, 0, -1)) for d in pair]
    order = list(dict.fromkeys(order))
    total = dot(x_ref[...], weight_rows(0), ((1,), (0,)))
    for d in order:
        x_in[d].wait_recv()
        total = total + dot(xall[d], weight_rows(d), ((1,), (0,)))
    yw[pl.ds(reach * rb, rb)] = total.astype(BF16).reshape(rb, fb, fw)
    y_in = [push(yw.at[pl.ds(reach * rb, rb)], yw.at[pl.ds((reach - o) * rb, rb)], "rows",
                 lax.rem(r + o + n, n)) for o in halo]
    for copy in y_in:
        copy.wait_recv()

    sums = [jnp.zeros((fb, fw), F32) for _ in range(rb)]
    for d in [0] + order:
        if d:
            t_in[d].wait_recv()
        for g in range(rb):
            for j in range(sl):
                at = (d * rb + g) * sl + j
                _, live, where = place[at]
                product = dot(tl[at], yw[jnp.minimum(where, yw.shape[0] - 1)], ((1,), (0,)))
                sums[g] = sums[g] + jnp.where(live, product, 0.0)
    pre = jnp.concatenate(sums, axis=0)
    hidden, slope = gelu_and_slope(pre)
    grad_pre = (ct_ref[...].astype(F32) * slope).astype(BF16)

    def piece(o):
        first = (reach + o) * rb
        parts = []
        for c in range(first, first + rb):
            tiles = jnp.concatenate([tl[inverse[c, g]] for g in range(rb)], axis=0)
            parts.append(dot(tiles, grad_pre, ((0,), (0,))))
        return jnp.concatenate(parts, axis=0)

    s_in = []
    for at, o in enumerate(reversed(halo)):
        sw[at] = piece(o).astype(BF16)
        s_in.append(push(sw.at[at], sr.at[at], "rows", lax.rem(r + o + n, n)))
    grad = piece(0)
    hid_ref[...] = hidden.astype(BF16)
    for at, copy in enumerate(s_in):
        copy.wait_recv()
        grad = grad + sr[at].astype(F32)
    gall[0] = grad.astype(BF16)
    g_in = {d: push(gall.at[0], gall.at[d], "feat", lax.rem(f + d, m)) for d in feat_d}

    for d in range(m):
        term = dot(xall[d] if d else x_ref[...], gall[0], ((0,), (0,)))
        at = pl.ds(pl.multiple_of(source[d] * fw, fw), fw)
        gpart[at, :] = term
        gwp[at, :] = term.astype(BF16)
    scale = float(rows * n) ** -0.5
    if in_sum:
        def chunk_of(d):
            return pl.ds(pl.multiple_of(lax.rem(r + n + d, n) * chunk, chunk), chunk)

        gw_in = {d: push(gwp.at[chunk_of(d)], gwr.at[d], "rows", lax.rem(r + d, n)) for d in row_d}
        part = gpart[chunk_of(0), :]
        for d in row_d:
            gw_in[d].wait_recv()
            part = part + gwr[d].astype(F32)
        gwa[0] = (part * scale).astype(BF16)
        all_in = {d: push(gwa.at[0], gwa.at[d], "rows", lax.rem(r + d, n)) for d in row_d}
    else:
        gw_ref[...] = gpart[...] * scale

    for d in feat_d:
        w_in[d].wait_recv()
    out = dot(gall[0], weight_rows(0), ((1,), (1,)))
    for d in order:
        g_in[d].wait_recv()
        out = out + dot(gall[d], wrow[d], ((1,), (1,)))
    gf_ref[...] = out.astype(BF16)
    if in_sum:
        gw_ref[chunk_of(0), :] = gwa[0].astype(F32)
        for d in row_d:
            all_in[d].wait_recv()
            gw_ref[chunk_of(-d), :] = gwa[d].astype(F32)
    for copy in started:
        copy.wait_send()


def on_device(features, weight, block_values, columns, counts, cotangent):
    n = lax.axis_size("rows")
    m = lax.axis_size("feat")
    reach = min(4, (n - 1) // 3)
    rb, sl, fb, _ = block_values.shape
    rows, fw = features.shape
    depth = weight.shape[0]
    in_sum = depth % (n * 16) == 0
    chunk = depth // n if in_sum else 16
    span = 2 * reach + 1
    copies = 4 * (m - 1) + 4 * reach + (2 * (n - 1) if in_sum else 0)
    vmem = pl.BlockSpec(memory_space=pltpu.VMEM)
    smem = pl.BlockSpec(memory_space=pltpu.SMEM)
    hidden, grad_features, grad_weight = pl.pallas_call(
        functools.partial(kernel, n, m, reach, rb, sl, in_sum),
        out_shape=(
            jax.ShapeDtypeStruct((rows, fw), BF16),
            jax.ShapeDtypeStruct((rows, fw), BF16),
            jax.ShapeDtypeStruct((depth, fw), F32),
        ),
        in_specs=[smem, smem, vmem, vmem, vmem, vmem],
        out_specs=(vmem, vmem, vmem),
        scratch_shapes=[
            pltpu.VMEM((m, rows, fw), BF16),
            pltpu.VMEM((m, fw, fw), BF16),
            pltpu.VMEM((m * rb * sl + 1, fb, fb), BF16),
            pltpu.VMEM((span * rb, fb, fw), BF16),
            pltpu.VMEM((2 * reach, rows, fw), BF16),
            pltpu.VMEM((2 * reach, rows, fw), BF16),
            pltpu.VMEM((m, rows, fw), BF16),
            pltpu.VMEM((depth, fw), F32),
            pltpu.VMEM((depth, fw), BF16),
            pltpu.VMEM((n if in_sum else 1, chunk, fw), BF16),
            pltpu.VMEM((n if in_sum else 1, chunk, fw), BF16),
            pltpu.SemaphoreType.DMA((copies,)),
            pltpu.SemaphoreType.DMA((copies,)),
        ],
        compiler_params=pltpu.CompilerParams(
            collective_id=0, has_side_effects=True, vmem_limit_bytes=32 * 1024 * 1024),
    )(columns, counts, features, weight, block_values.reshape(rb * sl, fb, fb), cotangent)
    if not in_sum:
        grad_weight = lax.psum(grad_weight, "rows")
    return hidden, grad_features, grad_weight


def solution(mesh):
    in_specs = (
        P("rows", "feat"),
        P(None, "feat"),
        P("rows", "feat", None, None),
        P("rows", None),
        P("rows"),
        P("rows", "feat"),
    )
    out_specs = (P("rows", "feat"), P("rows", "feat"), P(None, "feat"))
    return jax.shard_map(
        on_device, mesh=mesh, in_specs=in_specs, out_specs=out_specs, check_vma=False
    )
```

time: 142 us -> 45.1 us (0.32)
  blocking collectives: 56.9 us -> 0 us
  waiting for transfers between devices: 50.6 us -> 0 us
  Pallas kernels: 0 us -> 37.7 us
  between operations: 14.2 us -> 0.66 us
  starting transfers between devices: 9.58 us -> 0 us
  other arithmetic: 4.16 us -> 0 us
  local copies, waits for them, and re-layouts: 3.1 us -> 6.13 us
  matrix products: 2.89 us -> 0 us
    all_gather x4 -> x0, blocking collectives: 56.9 us -> none  [the longest x1 16.2 us: on_device(): panel_full = lax.all_gather(block_values, 'feat', axis=1, tiled=True)]
    psum x1 -> x0, waiting for transfers between devices: 47.4 us -> none  [on_device(): grad_weight = lax.psum(weight_terms, 'rows') * float(node_total) ** (-0.5)]
    pallas_call x0 -> x1, Pallas kernels: none -> 37.7 us  [on_device(): pl.pallas_call(functools.partial(kernel, n, m, reach, rb, sl, in_sum), ou...]
    ppermute x8 -> x0, starting transfers between devices: 9.54 us -> none  [shifted(): return lax.ppermute(value, axis, pairs)]
    unnamed x14 -> x15, local copies, waits for them, and re-layouts: 2.2 us -> 6.13 us
    ppermute x8 -> x0, waiting for transfers between devices: 3.23 us -> none  [shifted(): return lax.ppermute(value, axis, pairs)]
    dot_general x5 -> x0, matrix products: 2.89 us -> none  [the longest x1 0.97 us: on_device(): lax.dot_general(agg_full, grad_pre, (((0,), (0,)), ((), ())), preferred_e...]
    mul x1 -> x0, other arithmetic: 1.68 us -> none  [on_device(): grad_weight = lax.psum(weight_terms, 'rows') * float(node_total) ** (-0.5)]
  transfers between devices with their start and end apart: 9 -> 0, of which waited for: 4 -> 0; matrix products, arithmetic and copies ran while one was open for 2% -> 0% of each run, Pallas kernels for 0% -> 0%
where the time goes in v1:
time: 45.1 us; the launch traced here: 44.5 us
  Pallas kernels  37.7 us (84%)
  local copies, waits for them, and re-layouts  6.13 us (14%)
  between operations  0.66 us (1%)
    pallas_call x1, Pallas kernels, on_device(): pl.pallas_call(functools.partial(kernel, n, m, reach, rb, sl, in_sum), ou...  37.7 us
    unnamed x15, local copies, waits for them, and re-layouts  6.13 us

profile of v1, /device:TPU:0, one launch (start us, length us, event | category | flops | bytes accessed | tf_op | source)
XLA Modules:
  0.0 44.5 jit_solution(10297476403080936601)
XLA Ops:
  0.6 0.0 copy-start.5
  0.6 0.0 copy-start.4
  0.7 0.6 %copy-done.5 = s32[2]{0:T(128)S(1)} copy-done((s32[2]{0:T(128)S(1)}, s32[2]{0:T(128)}, u32[]{:S(2)}) %copy-start.5) | copy-done | bytes 32
  1.3 0.0 copy-done.4
  1.3 0.0 copy-start
  1.3 0.9 %copy-done = bf16[512,128]{1,0:T(8,128)(2,1)S(1)} copy-done((bf16[512,128]{1,0:T(8,128)(2,1)S(1)}, bf16[512,128]{1,0:T(8,128)(2,1)}, u32[]{:S(2)}) %copy-start) | copy-done | bytes 131096
  2.2 0.0 copy-start.1
  2.2 0.9 %copy-done.1 = bf16[2,2,128,128]{3,2,1,0:T(8,128)(2,1)S(1)} copy-done((bf16[2,2,128,128]{3,2,1,0:T(8,128)(2,1)S(1)}, bf16[2,2,128,128]{3,2,1,0:T(8,128)(2,1)}, u32[]{:S(2)}) %copy-start.1) | copy-done | bytes 131096
  3.1 0.0 copy-start.2
  3.1 0.8 %copy-done.2 = bf16[256,128]{1,0:T(8,128)(2,1)S(1)} copy-done((bf16[256,128]{1,0:T(8,128)(2,1)S(1)}, bf16[256,128]{1,0:T(8,128)(2,1)}, u32[]{:S(2)}) %copy-start.2) | copy-done | bytes 65560
  4.0 0.0 copy-start.3
  4.0 0.8 %copy-done.3 = bf16[256,128]{1,0:T(8,128)(2,1)S(1)} copy-done((bf16[256,128]{1,0:T(8,128)(2,1)S(1)}, bf16[256,128]{1,0:T(8,128)(2,1)}, u32[]{:S(2)}) %copy-start.3) | copy-done | bytes 65560
  4.8 37.7 %shard_map.85 = (bf16[256,128]{1,0:T(8,128)(2,1)S(1)}, bf16[256,128]{1,0:T(8,128)(2,1)S(1)}, f32[512,128]{1,0:T(8,128)S(1)}) custom-call(s32[2,8]{1,0:T(2,128)S(1)} %copy-done.4, s32[2]{0:T(128)S(1)} %copy-done.5, bf16[256,128]{1,0:T(8,128)(2,1)S(1)} %copy-done.2, bf16[512,128]{1,0:T(8,128)(2,1)S(1)} %copy-done, bf16[4,128,128]{2,1,0:T(8,128)(2,1)S(1)} %bitcast.1, ...), custom_call_target="tpu_custom_call" | custom-call | tf_op jit(solution)/shard_map/pallas_call | solution.py:192
  42.6 0.6 %copy.12 = bf16[256,128]{1,0:T(8,128)(2,1)} copy(bf16[256,128]{1,0:T(8,128)(2,1)S(1)} %get-tuple-element.6) | data formatting | bytes 131072
  43.2 0.6 %copy.13 = bf16[256,128]{1,0:T(8,128)(2,1)} copy(bf16[256,128]{1,0:T(8,128)(2,1)S(1)} %get-tuple-element.7) | data formatting | bytes 131072
  43.8 0.7 %copy.14 = f32[512,128]{1,0:T(8,128)} copy(f32[512,128]{1,0:T(8,128)S(1)} %get-tuple-element.8) | data formatting | bytes 524288
Async XLA Ops:
  0.6 0.7 %copy-start.5 = (s32[2]{0:T(128)S(1)}, s32[2]{0:T(128)}, u32[]{:S(2)}) copy-start(s32[2]{0:T(128)} %cnt.1) | copy-start | bytes 28
  0.6 0.7 %copy-start.4 = (s32[2,8]{1,0:T(2,128)S(1)}, s32[2,8]{1,0:T(2,128)}, u32[]{:S(2)}) copy-start(s32[2,8]{1,0:T(2,128)} %cols.1) | copy-start | bytes 196
  1.3 0.9 %copy-start = (bf16[512,128]{1,0:T(8,128)(2,1)S(1)}, bf16[512,128]{1,0:T(8,128)(2,1)}, u32[]{:S(2)}) copy-start(bf16[512,128]{1,0:T(8,128)(2,1)} %w_ref.1) | copy-start | bytes 393220
  2.2 0.9 %copy-start.1 = (bf16[2,2,128,128]{3,2,1,0:T(8,128)(2,1)S(1)}, bf16[2,2,128,128]{3,2,1,0:T(8,128)(2,1)}, u32[]{:S(2)}) copy-start(bf16[2,2,128,128]{3,2,1,0:T(8,128)(2,1)} %param.8) | copy-start | bytes 393220
  3.1 0.8 %copy-start.2 = (bf16[256,128]{1,0:T(8,128)(2,1)S(1)}, bf16[256,128]{1,0:T(8,128)(2,1)}, u32[]{:S(2)}) copy-start(bf16[256,128]{1,0:T(8,128)(2,1)} %x_ref.1) | copy-start | bytes 196612
  4.0 0.8 %copy-start.3 = (bf16[256,128]{1,0:T(8,128)(2,1)S(1)}, bf16[256,128]{1,0:T(8,128)(2,1)}, u32[]{:S(2)}) copy-start(bf16[256,128]{1,0:T(8,128)(2,1)} %ct_ref.1) | copy-start | bytes 196612

commit v2 on v1

v2 whole, which is shorter than its diff:
```python
import functools

import jax
import jax.numpy as jnp
from jax import lax
from jax.experimental import pallas as pl
from jax.experimental.pallas import tpu as pltpu
from jax.sharding import PartitionSpec as P

MESH = pl.DeviceIdType.MESH
F32 = jnp.float32
BF16 = jnp.bfloat16
GELU_SCALE = 0.7978845608028654
GELU_CUBE = 0.044715


def gelu_and_slope(v):
    square = v * v
    t = jnp.tanh(GELU_SCALE * (v + GELU_CUBE * (square * v)))
    half = 0.5 * (1.0 + t)
    inner = GELU_SCALE * (1.0 + 3.0 * GELU_CUBE * square)
    return v * half, half + 0.5 * v * (1.0 - t * t) * inner


def dot(a, b, contract):
    return lax.dot_general(a, b, (contract, ((), ())), preferred_element_type=F32)


def nearest_first(f, m):
    tables = []
    for me in range(m):
        line = [p for e in range(1, m) for p in (me - e, me + e) if 0 <= p < m]
        tables.append(line)
    steps = []
    for i in range(m - 1):
        at = jnp.int32(tables[0][i])
        for me in range(1, m):
            at = jnp.where(f == me, tables[me][i], at)
        steps.append(at)
    return steps


def kernel(n, m, reach, rb, sl, in_sum, cols_hbm, cnt_hbm, x_hbm, w_hbm, t_hbm, ct_hbm,
           hid_hbm, gf_hbm, gw_hbm, hid_ref, gf_ref, gw_ref, xall, w_ref, ct_ref, wrow, tl, yw, sw, sr, gall, gpart, gwp, gwr, gwa,
           send_sem, recv_sem, hop_send, hop_recv, load_sem, save_sem, cols, cnt):
    r = lax.axis_index("rows")
    f = lax.axis_index("feat")
    fb = t_hbm.shape[1]
    rows, fw = x_hbm.shape
    per = rb * sl
    chunk = gwr.shape[1]
    halo = [o for d in range(1, reach + 1) for o in (d, -d)]
    feat_d = list(range(1, m))
    row_d = list(range(1, n)) if in_sum else []
    row_peers = [d % n for d in (row_d if in_sum else halo)]

    def shard(s):
        return tl.at[pl.ds(s * per, per)]

    def rows_of(s):
        return pl.ds(pl.multiple_of(s * fw, fw), fw)

    loads = [
        pltpu.make_async_copy(x_hbm, xall.at[f], load_sem.at[0]),
        pltpu.make_async_copy(w_hbm, w_ref, load_sem.at[1]),
        pltpu.make_async_copy(t_hbm, shard(f), load_sem.at[2]),
        pltpu.make_async_copy(ct_hbm, ct_ref, load_sem.at[3]),
        pltpu.make_async_copy(w_hbm.at[rows_of(f)], wrow.at[f], load_sem.at[4]),
        pltpu.make_async_copy(cols_hbm, cols, load_sem.at[5]),
        pltpu.make_async_copy(cnt_hbm, cnt, load_sem.at[6]),
    ]
    for load in loads:
        load.start()

    barrier = pltpu.get_barrier_semaphore()
    for d in feat_d:
        pl.semaphore_signal(barrier, inc=1, device_id={"feat": lax.rem(f + d, m)}, device_id_type=MESH)
    for d in row_peers:
        pl.semaphore_signal(barrier, inc=1, device_id={"rows": lax.rem(r + d, n)}, device_id_type=MESH)
    pl.semaphore_wait(barrier, len(feat_d) + len(row_peers))

    started = []

    def push(src, dst, axis, peer):
        at = len(started)
        copy = pltpu.make_async_remote_copy(
            src_ref=src, dst_ref=dst, send_sem=send_sem.at[at], recv_sem=recv_sem.at[at],
            device_id={axis: peer}, device_id_type=MESH)
        copy.start()
        started.append(copy)
        return copy

    def hop(src, s, at, peer):
        return pltpu.make_async_remote_copy(
            src_ref=src, dst_ref=shard(s), send_sem=hop_send.at[at], recv_sem=hop_recv.at[s],
            device_id={"feat": peer}, device_id_type=MESH)

    x_in = {d: push(x_hbm, xall.at[f], "feat", lax.rem(f + d, m)) for d in feat_d}
    own_right = hop(t_hbm, f, 0, lax.rem(f + 1, m))
    own_left = hop(t_hbm, f, 1, lax.rem(f + m - 1, m))
    pl.when(f < m - 1)(own_right.start)
    pl.when(f > 0)(own_left.start)

    steps = nearest_first(f, m)
    forwards = []

    def receive(i):
        s = steps[i]
        hop(t_hbm, s, 0, f).wait_recv()
        right = hop(shard(s), s, 2 + i, lax.rem(f + 1, m))
        left = hop(shard(s), s, 2 + i, lax.rem(f + m - 1, m))
        to_right = jnp.logical_and(s < f, f < m - 1)
        to_left = jnp.logical_and(s > f, f > 0)
        pl.when(to_right)(right.start)
        pl.when(to_left)(left.start)
        forwards.append((to_right, right))
        forwards.append((to_left, left))

    loads[5].wait()
    loads[6].wait()
    zero_tile = m * per
    order = [f] + steps
    place = []
    for s in order:
        for g in range(rb):
            for j in range(sl):
                slot = s * sl + j
                col = cols[g, slot]
                offset = lax.rem(lax.div(col, rb) - r + reach + n, n)
                live = cnt[g] > slot
                where = offset * rb + lax.rem(col, rb)
                place.append((s, g, j, (s * rb + g) * sl + j, live, where))
    inverse = {}
    for c in range((2 * reach + 1) * rb):
        for g in range(rb):
            found = jnp.int32(zero_tile)
            for _, group, _, at, live, where in place:
                if group == g:
                    found = jnp.where(jnp.logical_and(live, where == c), at, found)
            inverse[c, g] = found
    tl[zero_tile] = jnp.zeros((fb, fb), BF16)

    loads[0].wait()
    loads[1].wait()
    total = dot(xall[f], w_ref[rows_of(f), :], ((1,), (0,)))
    for d in (1, m - 1) + tuple(range(2, m - 1)):
        k = lax.rem(f + m - d, m)
        x_in[d].wait_recv()
        total = total + dot(xall[k], w_ref[rows_of(k), :], ((1,), (0,)))
    yw[pl.ds(reach * rb, rb)] = total.astype(BF16).reshape(rb, fb, fw)
    y_in = [push(yw.at[pl.ds(reach * rb, rb)], yw.at[pl.ds((reach - o) * rb, rb)], "rows",
                 lax.rem(r + o + n, n)) for o in halo]
    for i in range(m - 2):
        receive(i)
    for copy in y_in:
        copy.wait_recv()
    loads[2].wait()

    sums = [jnp.zeros((fb, fw), F32) for _ in range(rb)]
    for i in range(m):
        if i == m - 1:
            receive(i - 1)
        for s, g, j, at, live, where in place[i * per:(i + 1) * per]:
            block = yw[jnp.minimum(where, yw.shape[0] - 1)]
            product = dot(tl[at], block, ((1,), (0,)))
            sums[g] = sums[g] + jnp.where(live, product, 0.0)
    w_in = [push(w_hbm.at[rows_of(lax.rem(f + d, m))], wrow.at[f], "feat", lax.rem(f + d, m)) for d in feat_d]
    pre = jnp.concatenate(sums, axis=0)
    hidden, slope = gelu_and_slope(pre)
    loads[3].wait()
    grad_pre = (ct_ref[...].astype(F32) * slope).astype(BF16)

    def spread(o, b):
        c = (reach + o) * rb + b
        tiles = jnp.concatenate([tl[inverse[c, g]] for g in range(rb)], axis=0)
        return dot(tiles, grad_pre, ((0,), (0,)))

    s_in = {}
    far_first = list(reversed(halo))
    for b in range(rb):
        for at, o in enumerate(far_first):
            sw[b, at] = spread(o, b).astype(BF16)
            s_in[b, at] = push(sw.at[b, at], sr.at[b, at], "rows", lax.rem(r + o + n, n))
    hid_ref[...] = hidden.astype(BF16)
    saves = [pltpu.make_async_copy(src, dst, save_sem.at[i]) for i, (src, dst) in enumerate(
        ((hid_ref, hid_hbm), (gf_ref, gf_hbm), (gw_ref, gw_hbm)))]
    saves[0].start()
    grads = [spread(0, b) for b in range(rb)]
    g_in = {}
    terms = [jnp.zeros((fw, fw), F32) for _ in range(m)]
    for b in range(rb):
        grad = grads[b]
        for at in range(len(far_first)):
            s_in[b, at].wait_recv()
            grad = grad + sr[b, at].astype(F32)
        grad = grad.astype(BF16)
        gall[b, f] = grad
        for d in feat_d:
            g_in[b, d] = push(gall.at[b, f], gall.at[b, f], "feat", lax.rem(f + d, m))
        for k in range(m):
            terms[k] = terms[k] + dot(xall[k, pl.ds(b * fb, fb), :], grad, ((0,), (0,)))
    for k in range(m):
        at = pl.ds(k * fw, fw)
        gpart[at, :] = terms[k]
        gwp[at, :] = terms[k].astype(BF16)
    scale = float(rows * n) ** -0.5
    if in_sum:
        def chunk_of(d):
            return pl.ds(pl.multiple_of(lax.rem(r + n + d, n) * chunk, chunk), chunk)

        gw_in = {d: push(gwp.at[chunk_of(d)], gwr.at[d], "rows", lax.rem(r + d, n)) for d in row_d}
        part = gpart[chunk_of(0), :]
        for d in row_d:
            gw_in[d].wait_recv()
            part = part + gwr[d].astype(F32)
        own_sum = (part * scale).astype(BF16)
        gwa[0] = own_sum
        all_in = {d: push(gwa.at[0], gwa.at[d], "rows", lax.rem(r + d, n)) for d in row_d}
        gw_ref[chunk_of(0), :] = own_sum.astype(F32)
    else:
        gw_ref[...] = gpart[...] * scale

    loads[4].wait()
    for copy in w_in:
        copy.wait_recv()
    for b in range(rb):
        for d in feat_d:
            g_in[b, d].wait_recv()
        out = jnp.zeros((fb, fw), F32)
        for k in range(m):
            out = out + dot(gall[b, k], wrow[k], ((1,), (1,)))
        gf_ref[pl.ds(b * fb, fb), :] = out.astype(BF16)
    saves[1].start()
    if in_sum:
        for d in row_d:
            all_in[d].wait_recv()
            gw_ref[chunk_of(-d), :] = gwa[d].astype(F32)
    saves[2].start()
    for copy in started:
        copy.wait_send()
    pl.when(f < m - 1)(own_right.wait_send)
    pl.when(f > 0)(own_left.wait_send)
    for sent, copy in forwards:
        pl.when(sent)(copy.wait_send)
    for save in saves:
        save.wait()


def store_kernel(a, b, c, a_out, b_out, c_out, sem):
    copies = [pltpu.make_async_copy(src, dst, sem.at[i])
              for i, (src, dst) in enumerate(((c, c_out), (a, a_out), (b, b_out)))]
    for copy in copies:
        copy.start()
    for copy in copies:
        copy.wait()


def on_device(features, weight, block_values, columns, counts, cotangent):
    n = lax.axis_size("rows")
    m = lax.axis_size("feat")
    reach = min(4, (n - 1) // 3)
    rb, sl, fb, _ = block_values.shape
    rows, fw = features.shape
    depth = weight.shape[0]
    in_sum = depth % (n * 16) == 0
    chunk = depth // n if in_sum else 16
    span = 2 * reach + 1
    copies = (2 + rb) * (m - 1) + (1 + rb) * 2 * reach + (2 * (n - 1) if in_sum else 0)
    hbm = pl.BlockSpec(memory_space=pltpu.HBM)
    hidden, grad_features, grad_weight = pl.pallas_call(
        functools.partial(kernel, n, m, reach, rb, sl, in_sum),
        out_shape=(
            jax.ShapeDtypeStruct((rows, fw), BF16),
            jax.ShapeDtypeStruct((rows, fw), BF16),
            jax.ShapeDtypeStruct((depth, fw), F32),
        ),
        in_specs=[hbm, hbm, hbm, hbm, hbm, hbm],
        out_specs=(hbm, hbm, hbm),
        scratch_shapes=[
            pltpu.VMEM((rows, fw), BF16),
            pltpu.VMEM((rows, fw), BF16),
            pltpu.VMEM((depth, fw), F32),
            pltpu.VMEM((m, rows, fw), BF16),
            pltpu.VMEM((depth, fw), BF16),
            pltpu.VMEM((rows, fw), BF16),
            pltpu.VMEM((m, fw, fw), BF16),
            pltpu.VMEM((m * rb * sl + 1, fb, fb), BF16),
            pltpu.VMEM((span * rb, fb, fw), BF16),
            pltpu.VMEM((rb, 2 * reach, fb, fw), BF16),
            pltpu.VMEM((rb, 2 * reach, fb, fw), BF16),
            pltpu.VMEM((rb, m, fb, fw), BF16),
            pltpu.VMEM((depth, fw), F32),
            pltpu.VMEM((depth, fw), BF16),
            pltpu.VMEM((n if in_sum else 1, chunk, fw), BF16),
            pltpu.VMEM((n if in_sum else 1, chunk, fw), BF16),
            pltpu.SemaphoreType.DMA((copies,)),
            pltpu.SemaphoreType.DMA((copies,)),
            pltpu.SemaphoreType.DMA((m + 1,)),
            pltpu.SemaphoreType.DMA((m,)),
            pltpu.SemaphoreType.DMA((7,)),
            pltpu.SemaphoreType.DMA((3,)),
            pltpu.SMEM(columns.shape, jnp.int32),
            pltpu.SMEM(counts.shape, jnp.int32),
        ],
        compiler_params=pltpu.CompilerParams(
            collective_id=0, has_side_effects=True, vmem_limit_bytes=56 * 1024 * 1024),
    )(columns, counts, features, weight, block_values.reshape(rb * sl, fb, fb), cotangent)
    if not in_sum:
        grad_weight = lax.psum(grad_weight, "rows")
    results = (hidden, grad_features, grad_weight)
    return pl.pallas_call(
        store_kernel,
        out_shape=tuple(jax.ShapeDtypeStruct(v.shape, v.dtype) for v in results),
        in_specs=[hbm] * 3,
        out_specs=(hbm,) * 3,
        scratch_shapes=[pltpu.SemaphoreType.DMA((3,))],
        compiler_params=pltpu.CompilerParams(vmem_limit_bytes=56 * 1024 * 1024),
    )(*results)


def solution(mesh):
    in_specs = (
        P("rows", "feat"),
        P(None, "feat"),
        P("rows", "feat", None, None),
        P("rows", None),
        P("rows"),
        P("rows", "feat"),
    )
    out_specs = (P("rows", "feat"), P("rows", "feat"), P(None, "feat"))
    return jax.shard_map(
        on_device, mesh=mesh, in_specs=in_specs, out_specs=out_specs, check_vma=False
    )
```

time: 45.1 us -> 51.7 us (1.15)
  Pallas kernels: 37.7 us -> 50.9 us
  local copies, waits for them, and re-layouts: 6.13 us -> 0 us
    pallas_call x0 -> x1, Pallas kernels: none -> 13 us  [on_device(): pl.pallas_call(store_kernel, out_shape=tuple((jax.ShapeDtypeStruct(v.shap...]
    unnamed x15 -> x0, local copies, waits for them, and re-layouts: 6.13 us -> none
where the time goes in v2:
time: 51.7 us; the launch traced here: 51.6 us
  Pallas kernels  50.9 us (98%)
  between operations  0.64 us (1%)
    pallas_call x1, Pallas kernels, on_device(): pl.pallas_call(functools.partial(kernel, n, m, reach, rb, sl, in_sum), ou...  37.9 us
    pallas_call x1, Pallas kernels, on_device(): pl.pallas_call(store_kernel, out_shape=tuple((jax.ShapeDtypeStruct(v.shap...  13 us

profile of v2, /device:TPU:0, one launch (start us, length us, event | category | flops | bytes accessed | tf_op | source)
XLA Modules:
  0.0 51.6 jit_solution(3967534968873345144)
XLA Ops:
  0.6 37.9 %shard_map.85 = (bf16[256,128]{1,0:T(8,128)(2,1)}, bf16[256,128]{1,0:T(8,128)(2,1)}, f32[512,128]{1,0:T(8,128)}) custom-call(s32[2,8]{1,0:T(2,128)} %cols_hbm.1, s32[2]{0:T(128)} %cnt_hbm.1, bf16[256,128]{1,0:T(8,128)(2,1)} %x_hbm.1, bf16[512,128]{1,0:T(8,128)(2,1)} %w_hbm.1, bf16[4,128,128]{2,1,0:T(8,128)(2,1)} %bitcast.1, bf16[256,128]{1,0:T(8,128)(2,1)} %ct_hbm.1), custom_call_target="tpu_custom_call" | custom-call | tf_op jit(solution)/shard_map/pallas_call | solution.py:270
  38.5 13.0 %shard_map.86 = (bf16[256,128]{1,0:T(8,128)(2,1)}, bf16[256,128]{1,0:T(8,128)(2,1)}, f32[512,128]{1,0:T(8,128)}) custom-call(bf16[256,128]{1,0:T(8,128)(2,1)} %get-tuple-element.6.a, bf16[256,128]{1,0:T(8,128)(2,1)} %get-tuple-element.7.b, f32[512,128]{1,0:T(8,128)} %get-tuple-element.8.c), custom_call_target="tpu_custom_call" | custom-call | tf_op jit(solution)/shard_map/pallas_call | solution.py:311

commit v3 on v2

--- a/solution.py
+++ b/solution.py
@@ -41,8 +41,8 @@
 
 
 def kernel(n, m, reach, rb, sl, in_sum, cols_hbm, cnt_hbm, x_hbm, w_hbm, t_hbm, ct_hbm,
-           hid_hbm, gf_hbm, gw_hbm, hid_ref, gf_ref, gw_ref, xall, w_ref, ct_ref, wrow, tl, yw, sw, sr, gall, gpart, gwp, gwr, gwa,
-           send_sem, recv_sem, hop_send, hop_recv, load_sem, save_sem, cols, cnt):
+           hid_ref, gf_ref, gw_ref, xall, w_ref, ct_ref, wrow, tl, yw, sw, sr, gall, gpart, gwp, gwr, gwa,
+           send_sem, recv_sem, hop_send, hop_recv, load_sem, cols, cnt):
     r = lax.axis_index("rows")
     f = lax.axis_index("feat")
     fb = t_hbm.shape[1]
@@ -182,9 +182,6 @@
             sw[b, at] = spread(o, b).astype(BF16)
             s_in[b, at] = push(sw.at[b, at], sr.at[b, at], "rows", lax.rem(r + o + n, n))
     hid_ref[...] = hidden.astype(BF16)
-    saves = [pltpu.make_async_copy(src, dst, save_sem.at[i]) for i, (src, dst) in enumerate(
-        ((hid_ref, hid_hbm), (gf_ref, gf_hbm), (gw_ref, gw_hbm)))]
-    saves[0].start()
     grads = [spread(0, b) for b in range(rb)]
     g_in = {}
     terms = [jnp.zeros((fw, fw), F32) for _ in range(m)]
@@ -230,20 +227,16 @@
         for k in range(m):
             out = out + dot(gall[b, k], wrow[k], ((1,), (1,)))
         gf_ref[pl.ds(b * fb, fb), :] = out.astype(BF16)
-    saves[1].start()
     if in_sum:
         for d in row_d:
             all_in[d].wait_recv()
             gw_ref[chunk_of(-d), :] = gwa[d].astype(F32)
-    saves[2].start()
     for copy in started:
         copy.wait_send()
     pl.when(f < m - 1)(own_right.wait_send)
     pl.when(f > 0)(own_left.wait_send)
     for sent, copy in forwards:
         pl.when(sent)(copy.wait_send)
-    for save in saves:
-        save.wait()
 
 
 def store_kernel(a, b, c, a_out, b_out, c_out, sem):
@@ -266,20 +259,18 @@
     chunk = depth // n if in_sum else 16
     span = 2 * reach + 1
     copies = (2 + rb) * (m - 1) + (1 + rb) * 2 * reach + (2 * (n - 1) if in_sum else 0)
+    vmem = pl.BlockSpec(memory_space=pltpu.VMEM)
     hbm = pl.BlockSpec(memory_space=pltpu.HBM)
     hidden, grad_features, grad_weight = pl.pallas_call(
         functools.partial(kernel, n, m, reach, rb, sl, in_sum),
         out_shape=(
-            jax.ShapeDtypeStruct((rows, fw), BF16),
-            jax.ShapeDtypeStruct((rows, fw), BF16),
-            jax.ShapeDtypeStruct((depth, fw), F32),
-        ),
-        in_specs=[hbm, hbm, hbm, hbm, hbm, hbm],
-        out_specs=(hbm, hbm, hbm),
-        scratch_shapes=[
             pltpu.VMEM((rows, fw), BF16),
             pltpu.VMEM((rows, fw), BF16),
             pltpu.VMEM((depth, fw), F32),
+        ),
+        in_specs=[hbm, hbm, hbm, hbm, hbm, hbm],
+        out_specs=(vmem, vmem, vmem),
+        scratch_shapes=[
             pltpu.VMEM((m, rows, fw), BF16),
             pltpu.VMEM((depth, fw), BF16),
             pltpu.VMEM((rows, fw), BF16),
@@ -298,23 +289,23 @@
             pltpu.SemaphoreType.DMA((m + 1,)),
             pltpu.SemaphoreType.DMA((m,)),
             pltpu.SemaphoreType.DMA((7,)),
-            pltpu.SemaphoreType.DMA((3,)),
             pltpu.SMEM(columns.shape, jnp.int32),
             pltpu.SMEM(counts.shape, jnp.int32),
         ],
         compiler_params=pltpu.CompilerParams(
-            collective_id=0, has_side_effects=True, vmem_limit_bytes=56 * 1024 * 1024),
-    )(columns, counts, features, weight, block_values.reshape(rb * sl, fb, fb), cotangent)
+            collective_id=0, has_side_effects=True, vmem_limit_bytes=32 * 1024 * 1024),
+    )(*(pltpu.with_memory_space_constraint(v, pltpu.HBM) for v in (
+        columns, counts, features, weight, block_values.reshape(rb * sl, fb, fb), cotangent)))
     if not in_sum:
         grad_weight = lax.psum(grad_weight, "rows")
     results = (hidden, grad_features, grad_weight)
     return pl.pallas_call(
         store_kernel,
         out_shape=tuple(jax.ShapeDtypeStruct(v.shape, v.dtype) for v in results),
-        in_specs=[hbm] * 3,
+        in_specs=[vmem] * 3,
         out_specs=(hbm,) * 3,
         scratch_shapes=[pltpu.SemaphoreType.DMA((3,))],
-        compiler_params=pltpu.CompilerParams(vmem_limit_bytes=56 * 1024 * 1024),
+        compiler_params=pltpu.CompilerParams(vmem_limit_bytes=32 * 1024 * 1024),
     )(*results)
 
 

time: 51.7 us -> 38.8 us (0.75)
  Pallas kernels: 50.9 us -> 38 us
    pallas_call x1, Pallas kernels: 13 us -> 0.76 us  [on_device(): pl.pallas_call(store_kernel, out_shape=tuple((jax.ShapeDtypeStruct(v.shap...]
    pallas_call x1, Pallas kernels: 37.9 us -> 37.2 us  [on_device(): pl.pallas_call(functools.partial(kernel, n, m, reach, rb, sl, in_sum), ou...]
where the time goes in v3:
time: 38.8 us; the launch traced here: 38.6 us
  Pallas kernels  38 us (98%)
  between operations  0.64 us (2%)
    pallas_call x1, Pallas kernels, on_device(): pl.pallas_call(functools.partial(kernel, n, m, reach, rb, sl, in_sum), ou...  37.2 us

profile of v3, /device:TPU:0, one launch (start us, length us, event | category | flops | bytes accessed | tf_op | source)
XLA Modules:
  0.0 38.6 jit_solution(12911632227462170369)
XLA Ops:
  0.6 37.2 %shard_map.85 = (bf16[256,128]{1,0:T(8,128)(2,1)S(1)}, bf16[256,128]{1,0:T(8,128)(2,1)S(1)}, f32[512,128]{1,0:T(8,128)S(1)}) custom-call(s32[2,8]{1,0:T(2,128)} %cols_hbm.1, s32[2]{0:T(128)} %cnt_hbm.1, bf16[256,128]{1,0:T(8,128)(2,1)} %x_hbm.1, bf16[512,128]{1,0:T(8,128)(2,1)} %w_hbm.1, bf16[4,128,128]{2,1,0:T(8,128)(2,1)} %bitcast.1, bf16[256,128]{1,0:T(8,128)(2,1)} %ct_hbm.1), custom_call_target="tpu_custom_call" | custom-call | tf_op jit(solution)/shard_map/pallas_call | solution.py:264
  37.9 0.8 %shard_map.86 = (bf16[256,128]{1,0:T(8,128)(2,1)}, bf16[256,128]{1,0:T(8,128)(2,1)}, f32[512,128]{1,0:T(8,128)}) custom-call(bf16[256,128]{1,0:T(8,128)(2,1)S(1)} %get-tuple-element.6.a, bf16[256,128]{1,0:T(8,128)(2,1)S(1)} %get-tuple-element.7.b, f32[512,128]{1,0:T(8,128)S(1)} %get-tuple-element.8.c), custom_call_target="tpu_custom_call" | custom-call | tf_op jit(solution)/shard_map/pallas_call | solution.py:302

commit v4 on v3

--- a/solution.py
+++ b/solution.py
@@ -41,8 +41,9 @@
 
 
 def kernel(n, m, reach, rb, sl, in_sum, cols_hbm, cnt_hbm, x_hbm, w_hbm, t_hbm, ct_hbm,
-           hid_ref, gf_ref, gw_ref, xall, w_ref, ct_ref, wrow, tl, yw, sw, sr, gall, gpart, gwp, gwr, gwa,
+           hid_ref, gf_ref, gw_ref, xall, w_ref, ct_ref, wrow, tl, tl_t, x_t, yw, sw, sr, gall, gpart, gwp, gwr, gwa,
            send_sem, recv_sem, hop_send, hop_recv, load_sem, cols, cnt):
+
     r = lax.axis_index("rows")
     f = lax.axis_index("feat")
     fb = t_hbm.shape[1]
@@ -90,31 +91,33 @@
         started.append(copy)
         return copy
 
-    def hop(src, s, at, peer):
+    def slot_of(kind, s):
+        return shard(s) if kind else xall.at[s]
+
+    def hop(kind, src, s, at, peer):
         return pltpu.make_async_remote_copy(
-            src_ref=src, dst_ref=shard(s), send_sem=hop_send.at[at], recv_sem=hop_recv.at[s],
-            device_id={"feat": peer}, device_id_type=MESH)
-
-    x_in = {d: push(x_hbm, xall.at[f], "feat", lax.rem(f + d, m)) for d in feat_d}
-    own_right = hop(t_hbm, f, 0, lax.rem(f + 1, m))
-    own_left = hop(t_hbm, f, 1, lax.rem(f + m - 1, m))
-    pl.when(f < m - 1)(own_right.start)
-    pl.when(f > 0)(own_left.start)
-
-    steps = nearest_first(f, m)
+            src_ref=src, dst_ref=slot_of(kind, s), send_sem=hop_send.at[kind, at],
+            recv_sem=hop_recv.at[kind, s], device_id={"feat": peer}, device_id_type=MESH)
+
     forwards = []
 
-    def receive(i):
-        s = steps[i]
-        hop(t_hbm, s, 0, f).wait_recv()
-        right = hop(shard(s), s, 2 + i, lax.rem(f + 1, m))
-        left = hop(shard(s), s, 2 + i, lax.rem(f + m - 1, m))
-        to_right = jnp.logical_and(s < f, f < m - 1)
-        to_left = jnp.logical_and(s > f, f > 0)
+    def onward(kind, src, s, at, to_right, to_left):
+        right = hop(kind, src, s, at, lax.rem(f + 1, m))
+        left = hop(kind, src, s, at + 1, lax.rem(f + m - 1, m))
         pl.when(to_right)(right.start)
         pl.when(to_left)(left.start)
         forwards.append((to_right, right))
         forwards.append((to_left, left))
+
+    for kind, src in enumerate((x_hbm, t_hbm)):
+        onward(kind, src, f, 0, f < m - 1, f > 0)
+    steps = nearest_first(f, m)
+
+    def receive(kind, i):
+        s = steps[i]
+        hop(kind, slot_of(kind, s), s, 0, lax.rem(f + 1, m)).wait_recv()
+        onward(kind, slot_of(kind, s), s, 2 + 2 * i, jnp.logical_and(s < f, f < m - 1),
+               jnp.logical_and(s > f, f > 0))
 
     loads[5].wait()
     loads[6].wait()
@@ -138,20 +141,21 @@
                 if group == g:
                     found = jnp.where(jnp.logical_and(live, where == c), at, found)
             inverse[c, g] = found
-    tl[zero_tile] = jnp.zeros((fb, fb), BF16)
+    tl_t[zero_tile] = jnp.zeros((fb, fb), BF16)
 
     loads[0].wait()
     loads[1].wait()
     total = dot(xall[f], w_ref[rows_of(f), :], ((1,), (0,)))
-    for d in (1, m - 1) + tuple(range(2, m - 1)):
-        k = lax.rem(f + m - d, m)
-        x_in[d].wait_recv()
+    for i, k in enumerate(steps):
+        receive(0, i)
         total = total + dot(xall[k], w_ref[rows_of(k), :], ((1,), (0,)))
     yw[pl.ds(reach * rb, rb)] = total.astype(BF16).reshape(rb, fb, fw)
     y_in = [push(yw.at[pl.ds(reach * rb, rb)], yw.at[pl.ds((reach - o) * rb, rb)], "rows",
                  lax.rem(r + o + n, n)) for o in halo]
+    for k in range(m):
+        x_t[k] = xall[k].T
     for i in range(m - 2):
-        receive(i)
+        receive(1, i)
     for copy in y_in:
         copy.wait_recv()
     loads[2].wait()
@@ -159,11 +163,12 @@
     sums = [jnp.zeros((fb, fw), F32) for _ in range(rb)]
     for i in range(m):
         if i == m - 1:
-            receive(i - 1)
+            receive(1, i - 1)
         for s, g, j, at, live, where in place[i * per:(i + 1) * per]:
             block = yw[jnp.minimum(where, yw.shape[0] - 1)]
             product = dot(tl[at], block, ((1,), (0,)))
             sums[g] = sums[g] + jnp.where(live, product, 0.0)
+            tl_t[at] = tl[at].T
     w_in = [push(w_hbm.at[rows_of(lax.rem(f + d, m))], wrow.at[f], "feat", lax.rem(f + d, m)) for d in feat_d]
     pre = jnp.concatenate(sums, axis=0)
     hidden, slope = gelu_and_slope(pre)
@@ -172,8 +177,8 @@
 
     def spread(o, b):
         c = (reach + o) * rb + b
-        tiles = jnp.concatenate([tl[inverse[c, g]] for g in range(rb)], axis=0)
-        return dot(tiles, grad_pre, ((0,), (0,)))
+        tiles = jnp.concatenate([tl_t[inverse[c, g]] for g in range(rb)], axis=1)
+        return dot(tiles, grad_pre, ((1,), (0,)))
 
     s_in = {}
     far_first = list(reversed(halo))
@@ -195,7 +200,7 @@
         for d in feat_d:
             g_in[b, d] = push(gall.at[b, f], gall.at[b, f], "feat", lax.rem(f + d, m))
         for k in range(m):
-            terms[k] = terms[k] + dot(xall[k, pl.ds(b * fb, fb), :], grad, ((0,), (0,)))
+            terms[k] = terms[k] + dot(x_t[k, :, pl.ds(b * fb, fb)], grad, ((1,), (0,)))
     for k in range(m):
         at = pl.ds(k * fw, fw)
         gpart[at, :] = terms[k]
@@ -233,8 +238,6 @@
             gw_ref[chunk_of(-d), :] = gwa[d].astype(F32)
     for copy in started:
         copy.wait_send()
-    pl.when(f < m - 1)(own_right.wait_send)
-    pl.when(f > 0)(own_left.wait_send)
     for sent, copy in forwards:
         pl.when(sent)(copy.wait_send)
 
@@ -258,7 +261,7 @@
     in_sum = depth % (n * 16) == 0
     chunk = depth // n if in_sum else 16
     span = 2 * reach + 1
-    copies = (2 + rb) * (m - 1) + (1 + rb) * 2 * reach + (2 * (n - 1) if in_sum else 0)
+    copies = (1 + rb) * (m - 1) + (1 + rb) * 2 * reach + (2 * (n - 1) if in_sum else 0)
     vmem = pl.BlockSpec(memory_space=pltpu.VMEM)
     hbm = pl.BlockSpec(memory_space=pltpu.HBM)
     hidden, grad_features, grad_weight = pl.pallas_call(
@@ -275,7 +278,9 @@
             pltpu.VMEM((depth, fw), BF16),
             pltpu.VMEM((rows, fw), BF16),
             pltpu.VMEM((m, fw, fw), BF16),
+            pltpu.VMEM((m * rb * sl, fb, fb), BF16),
             pltpu.VMEM((m * rb * sl + 1, fb, fb), BF16),
+            pltpu.VMEM((m, fw, rows), BF16),
             pltpu.VMEM((span * rb, fb, fw), BF16),
             pltpu.VMEM((rb, 2 * reach, fb, fw), BF16),
             pltpu.VMEM((rb, 2 * reach, fb, fw), BF16),
@@ -286,8 +291,8 @@
             pltpu.VMEM((n if in_sum else 1, chunk, fw), BF16),
             pltpu.SemaphoreType.DMA((copies,)),
             pltpu.SemaphoreType.DMA((copies,)),
-            pltpu.SemaphoreType.DMA((m + 1,)),
-            pltpu.SemaphoreType.DMA((m,)),
+            pltpu.SemaphoreType.DMA((2, 2 * m)),
+            pltpu.SemaphoreType.DMA((2, m)),
             pltpu.SemaphoreType.DMA((7,)),
             pltpu.SMEM(columns.shape, jnp.int32),
             pltpu.SMEM(counts.shape, jnp.int32),

time: 38.8 us -> 38.2 us (0.985)
  Pallas kernels: 38 us -> 37.5 us
    pallas_call x1, Pallas kernels: 37.2 us -> 36.7 us  [on_device(): pl.pallas_call(functools.partial(kernel, n, m, reach, rb, sl, in_sum), ou...]
where the time goes in v4:
time: 38.2 us; the launch traced here: 38.1 us
  Pallas kernels  37.5 us (98%)
  between operations  0.64 us (2%)
    pallas_call x1, Pallas kernels, on_device(): pl.pallas_call(functools.partial(kernel, n, m, reach, rb, sl, in_sum), ou...  36.7 us
    pallas_call x1, Pallas kernels, on_device(): pl.pallas_call(store_kernel, out_shape=tuple((jax.ShapeDtypeStruct(v.shap...  0.76 us

profile of v4, /device:TPU:0, one launch (start us, length us, event | category | flops | bytes accessed | tf_op | source)
XLA Modules:
  0.0 38.1 jit_solution(8104500340241883001)
XLA Ops:
  0.6 36.7 %shard_map.85 = (bf16[256,128]{1,0:T(8,128)(2,1)S(1)}, bf16[256,128]{1,0:T(8,128)(2,1)S(1)}, f32[512,128]{1,0:T(8,128)S(1)}) custom-call(s32[2,8]{1,0:T(2,128)} %cols_hbm.1, s32[2]{0:T(128)} %cnt_hbm.1, bf16[256,128]{1,0:T(8,128)(2,1)} %x_hbm.1, bf16[512,128]{1,0:T(8,128)(2,1)} %w_hbm.1, bf16[4,128,128]{2,1,0:T(8,128)(2,1)} %bitcast.1, bf16[256,128]{1,0:T(8,128)(2,1)} %ct_hbm.1), custom_call_target="tpu_custom_call" | custom-call | tf_op jit(solution)/shard_map/pallas_call | solution.py:267
  37.3 0.8 %shard_map.86 = (bf16[256,128]{1,0:T(8,128)(2,1)}, bf16[256,128]{1,0:T(8,128)(2,1)}, f32[512,128]{1,0:T(8,128)}) custom-call(bf16[256,128]{1,0:T(8,128)(2,1)S(1)} %get-tuple-element.6.a, bf16[256,128]{1,0:T(8,128)(2,1)S(1)} %get-tuple-element.7.b, f32[512,128]{1,0:T(8,128)S(1)} %get-tuple-element.8.c), custom_call_target="tpu_custom_call" | custom-call | tf_op jit(solution)/shard_map/pallas_call | solution.py:307

commit v5 on v4

--- a/solution.py
+++ b/solution.py
@@ -41,7 +41,7 @@
 
 
 def kernel(n, m, reach, rb, sl, in_sum, cols_hbm, cnt_hbm, x_hbm, w_hbm, t_hbm, ct_hbm,
-           hid_ref, gf_ref, gw_ref, xall, w_ref, ct_ref, wrow, tl, tl_t, x_t, yw, sw, sr, gall, gpart, gwp, gwr, gwa,
+           hid_ref, gf_ref, gw_ref, xall, w_ref, ct_ref, wrow, w_t, tl, tl_t, x_t, yw, sw, sr, gall, gpart, gwp, gwr, gwa,
            send_sem, recv_sem, hop_send, hop_recv, load_sem, cols, cnt):
 
     r = lax.axis_index("rows")
@@ -92,7 +92,7 @@
         return copy
 
     def slot_of(kind, s):
-        return shard(s) if kind else xall.at[s]
+        return tl.at[pl.ds((s * rb + kind - 1) * sl, sl)] if kind else xall.at[s]
 
     def hop(kind, src, s, at, peer):
         return pltpu.make_async_remote_copy(
@@ -109,7 +109,7 @@
         forwards.append((to_right, right))
         forwards.append((to_left, left))
 
-    for kind, src in enumerate((x_hbm, t_hbm)):
+    for kind, src in enumerate([x_hbm] + [t_hbm.at[pl.ds(g * sl, sl)] for g in range(rb)]):
         onward(kind, src, f, 0, f < m - 1, f > 0)
     steps = nearest_first(f, m)
 
@@ -153,22 +153,29 @@
     y_in = [push(yw.at[pl.ds(reach * rb, rb)], yw.at[pl.ds((reach - o) * rb, rb)], "rows",
                  lax.rem(r + o + n, n)) for o in halo]
     for k in range(m):
-        x_t[k] = xall[k].T
+        x_t[pl.ds(k * fw, fw), :] = xall[k].T
     for i in range(m - 2):
-        receive(1, i)
+        for g in range(rb):
+            receive(1 + g, i)
     for copy in y_in:
         copy.wait_recv()
     loads[2].wait()
 
     sums = [jnp.zeros((fb, fw), F32) for _ in range(rb)]
-    for i in range(m):
-        if i == m - 1:
-            receive(1, i - 1)
-        for s, g, j, at, live, where in place[i * per:(i + 1) * per]:
-            block = yw[jnp.minimum(where, yw.shape[0] - 1)]
-            product = dot(tl[at], block, ((1,), (0,)))
-            sums[g] = sums[g] + jnp.where(live, product, 0.0)
-            tl_t[at] = tl[at].T
+    def add(groups, first, last):
+        for g in groups:
+            mine = [p for p in place[first * per:last * per] if p[1] == g]
+            tiles = [tl[at] for _, _, _, at, _, _ in mine]
+            blocks = [jnp.where(live, yw[jnp.minimum(where, yw.shape[0] - 1)], jnp.zeros((), BF16))
+                      for _, _, _, _, live, where in mine]
+            sums[g] = sums[g] + dot(jnp.concatenate(tiles, axis=1), jnp.concatenate(blocks, axis=0), ((1,), (0,)))
+            for tile, (_, _, _, at, _, _) in zip(tiles, mine):
+                tl_t[at] = tile.T
+
+    add(range(rb), 0, m - 1)
+    for g in range(rb):
+        receive(1 + g, m - 2)
+        add([g], m - 1, m)
     w_in = [push(w_hbm.at[rows_of(lax.rem(f + d, m))], wrow.at[f], "feat", lax.rem(f + d, m)) for d in feat_d]
     pre = jnp.concatenate(sums, axis=0)
     hidden, slope = gelu_and_slope(pre)
@@ -188,8 +195,12 @@
             s_in[b, at] = push(sw.at[b, at], sr.at[b, at], "rows", lax.rem(r + o + n, n))
     hid_ref[...] = hidden.astype(BF16)
     grads = [spread(0, b) for b in range(rb)]
+    loads[4].wait()
+    for copy in w_in:
+        copy.wait_recv()
+    for k in range(m):
+        w_t[pl.ds(k * fw, fw), :] = wrow[k].T
     g_in = {}
-    terms = [jnp.zeros((fw, fw), F32) for _ in range(m)]
     for b in range(rb):
         grad = grads[b]
         for at in range(len(far_first)):
@@ -199,12 +210,10 @@
         gall[b, f] = grad
         for d in feat_d:
             g_in[b, d] = push(gall.at[b, f], gall.at[b, f], "feat", lax.rem(f + d, m))
-        for k in range(m):
-            terms[k] = terms[k] + dot(x_t[k, :, pl.ds(b * fb, fb)], grad, ((1,), (0,)))
-    for k in range(m):
-        at = pl.ds(k * fw, fw)
-        gpart[at, :] = terms[k]
-        gwp[at, :] = terms[k].astype(BF16)
+        grads[b] = grad
+    terms = dot(x_t[...], jnp.concatenate(grads, axis=0), ((1,), (0,)))
+    gwp[...] = terms.astype(BF16)
+    gpart[...] = terms
     scale = float(rows * n) ** -0.5
     if in_sum:
         def chunk_of(d):
@@ -222,15 +231,10 @@
     else:
         gw_ref[...] = gpart[...] * scale
 
-    loads[4].wait()
-    for copy in w_in:
-        copy.wait_recv()
     for b in range(rb):
         for d in feat_d:
             g_in[b, d].wait_recv()
-        out = jnp.zeros((fb, fw), F32)
-        for k in range(m):
-            out = out + dot(gall[b, k], wrow[k], ((1,), (1,)))
+        out = dot(jnp.concatenate([gall[b, k] for k in range(m)], axis=1), w_t[...], ((1,), (0,)))
         gf_ref[pl.ds(b * fb, fb), :] = out.astype(BF16)
     if in_sum:
         for d in row_d:
@@ -278,9 +282,10 @@
             pltpu.VMEM((depth, fw), BF16),
             pltpu.VMEM((rows, fw), BF16),
             pltpu.VMEM((m, fw, fw), BF16),
+            pltpu.VMEM((m * fw, fw), BF16),
             pltpu.VMEM((m * rb * sl, fb, fb), BF16),
             pltpu.VMEM((m * rb * sl + 1, fb, fb), BF16),
-            pltpu.VMEM((m, fw, rows), BF16),
+            pltpu.VMEM((m * fw, rows), BF16),
             pltpu.VMEM((span * rb, fb, fw), BF16),
             pltpu.VMEM((rb, 2 * reach, fb, fw), BF16),
             pltpu.VMEM((rb, 2 * reach, fb, fw), BF16),
@@ -291,8 +296,8 @@
             pltpu.VMEM((n if in_sum else 1, chunk, fw), BF16),
             pltpu.SemaphoreType.DMA((copies,)),
             pltpu.SemaphoreType.DMA((copies,)),
-            pltpu.SemaphoreType.DMA((2, 2 * m)),
-            pltpu.SemaphoreType.DMA((2, m)),
+            pltpu.SemaphoreType.DMA((1 + rb, 2 * m)),
+            pltpu.SemaphoreType.DMA((1 + rb, m)),
             pltpu.SemaphoreType.DMA((7,)),
             pltpu.SMEM(columns.shape, jnp.int32),
             pltpu.SMEM(counts.shape, jnp.int32),

time: 38.2 us -> 38.4 us (level)
  no operation moved by 1% of the time
where the time goes in v5:
time: 38.4 us; the launch traced here: 38.2 us
  Pallas kernels  37.6 us (98%)
  between operations  0.64 us (2%)
    pallas_call x1, Pallas kernels, on_device(): pl.pallas_call(functools.partial(kernel, n, m, reach, rb, sl, in_sum), ou...  36.8 us

profile of v5, /device:TPU:0, one launch (start us, length us, event | category | flops | bytes accessed | tf_op | source)
XLA Modules:
  0.0 38.2 jit_solution(4723955666360486984)
XLA Ops:
  0.6 36.8 %shard_map.85 = (bf16[256,128]{1,0:T(8,128)(2,1)S(1)}, bf16[256,128]{1,0:T(8,128)(2,1)S(1)}, f32[512,128]{1,0:T(8,128)S(1)}) custom-call(s32[2,8]{1,0:T(2,128)} %cols_hbm.1, s32[2]{0:T(128)} %cnt_hbm.1, bf16[256,128]{1,0:T(8,128)(2,1)} %x_hbm.1, bf16[512,128]{1,0:T(8,128)(2,1)} %w_hbm.1, bf16[4,128,128]{2,1,0:T(8,128)(2,1)} %bitcast.1, bf16[256,128]{1,0:T(8,128)(2,1)} %ct_hbm.1), custom_call_target="tpu_custom_call" | custom-call | tf_op jit(solution)/shard_map/pallas_call | solution.py:271
  37.4 0.8 %shard_map.86 = (bf16[256,128]{1,0:T(8,128)(2,1)}, bf16[256,128]{1,0:T(8,128)(2,1)}, f32[512,128]{1,0:T(8,128)}) custom-call(bf16[256,128]{1,0:T(8,128)(2,1)S(1)} %get-tuple-element.6.a, bf16[256,128]{1,0:T(8,128)(2,1)S(1)} %get-tuple-element.7.b, f32[512,128]{1,0:T(8,128)S(1)} %get-tuple-element.8.c), custom_call_target="tpu_custom_call" | custom-call | tf_op jit(solution)/shard_map/pallas_call | solution.py:312

commit v6 on v5

--- a/solution.py
+++ b/solution.py
@@ -119,6 +119,15 @@
         onward(kind, slot_of(kind, s), s, 2 + 2 * i, jnp.logical_and(s < f, f < m - 1),
                jnp.logical_and(s > f, f > 0))
 
+    loads[0].wait()
+    loads[1].wait()
+    total = dot(xall[f], w_ref[rows_of(f), :], ((1,), (0,)))
+    for i, k in enumerate(steps):
+        receive(0, i)
+        total = total + dot(xall[k], w_ref[rows_of(k), :], ((1,), (0,)))
+    yw[pl.ds(reach * rb, rb)] = total.astype(BF16).reshape(rb, fb, fw)
+    y_in = [push(yw.at[pl.ds(reach * rb, rb)], yw.at[pl.ds((reach - o) * rb, rb)], "rows",
+                 lax.rem(r + o + n, n)) for o in halo]
     loads[5].wait()
     loads[6].wait()
     zero_tile = m * per
@@ -143,17 +152,6 @@
             inverse[c, g] = found
     tl_t[zero_tile] = jnp.zeros((fb, fb), BF16)
 
-    loads[0].wait()
-    loads[1].wait()
-    total = dot(xall[f], w_ref[rows_of(f), :], ((1,), (0,)))
-    for i, k in enumerate(steps):
-        receive(0, i)
-        total = total + dot(xall[k], w_ref[rows_of(k), :], ((1,), (0,)))
-    yw[pl.ds(reach * rb, rb)] = total.astype(BF16).reshape(rb, fb, fw)
-    y_in = [push(yw.at[pl.ds(reach * rb, rb)], yw.at[pl.ds((reach - o) * rb, rb)], "rows",
-                 lax.rem(r + o + n, n)) for o in halo]
-    for k in range(m):
-        x_t[pl.ds(k * fw, fw), :] = xall[k].T
     for i in range(m - 2):
         for g in range(rb):
             receive(1 + g, i)
@@ -187,39 +185,39 @@
         tiles = jnp.concatenate([tl_t[inverse[c, g]] for g in range(rb)], axis=1)
         return dot(tiles, grad_pre, ((1,), (0,)))
 
-    s_in = {}
-    far_first = list(reversed(halo))
-    for b in range(rb):
-        for at, o in enumerate(far_first):
-            sw[b, at] = spread(o, b).astype(BF16)
-            s_in[b, at] = push(sw.at[b, at], sr.at[b, at], "rows", lax.rem(r + o + n, n))
+    s_in = []
+    for at, o in enumerate(reversed(halo)):
+        for b in range(rb):
+            sw[at, pl.ds(b * fb, fb), :] = spread(o, b).astype(BF16)
+        s_in.append(push(sw.at[at], sr.at[at], "rows", lax.rem(r + o + n, n)))
+    grad = jnp.concatenate([spread(0, b) for b in range(rb)], axis=0)
     hid_ref[...] = hidden.astype(BF16)
-    grads = [spread(0, b) for b in range(rb)]
+    for k in range(m):
+        x_t[pl.ds(k * fw, fw), :] = xall[k].T
     loads[4].wait()
     for copy in w_in:
         copy.wait_recv()
     for k in range(m):
         w_t[pl.ds(k * fw, fw), :] = wrow[k].T
-    g_in = {}
-    for b in range(rb):
-        grad = grads[b]
-        for at in range(len(far_first)):
-            s_in[b, at].wait_recv()
-            grad = grad + sr[b, at].astype(F32)
-        grad = grad.astype(BF16)
-        gall[b, f] = grad
-        for d in feat_d:
-            g_in[b, d] = push(gall.at[b, f], gall.at[b, f], "feat", lax.rem(f + d, m))
-        grads[b] = grad
-    terms = dot(x_t[...], jnp.concatenate(grads, axis=0), ((1,), (0,)))
+    for at, copy in enumerate(s_in):
+        copy.wait_recv()
+        grad = grad + sr[at].astype(F32)
+    grad = grad.astype(BF16)
+    gall[f] = grad
+    terms = dot(x_t[...], grad, ((1,), (0,)))
     gwp[...] = terms.astype(BF16)
     gpart[...] = terms
+
+    def gather_grad():
+        return [push(gall.at[f], gall.at[f], "feat", lax.rem(f + d, m)) for d in feat_d]
+
     scale = float(rows * n) ** -0.5
     if in_sum:
         def chunk_of(d):
             return pl.ds(pl.multiple_of(lax.rem(r + n + d, n) * chunk, chunk), chunk)
 
         gw_in = {d: push(gwp.at[chunk_of(d)], gwr.at[d], "rows", lax.rem(r + d, n)) for d in row_d}
+        g_in = gather_grad()
         part = gpart[chunk_of(0), :]
         for d in row_d:
             gw_in[d].wait_recv()
@@ -230,12 +228,12 @@
         gw_ref[chunk_of(0), :] = own_sum.astype(F32)
     else:
         gw_ref[...] = gpart[...] * scale
-
-    for b in range(rb):
-        for d in feat_d:
-            g_in[b, d].wait_recv()
-        out = dot(jnp.concatenate([gall[b, k] for k in range(m)], axis=1), w_t[...], ((1,), (0,)))
-        gf_ref[pl.ds(b * fb, fb), :] = out.astype(BF16)
+        g_in = gather_grad()
+
+    for copy in g_in:
+        copy.wait_recv()
+    out = dot(jnp.concatenate([gall[k] for k in range(m)], axis=1), w_t[...], ((1,), (0,)))
+    gf_ref[...] = out.astype(BF16)
     if in_sum:
         for d in row_d:
             all_in[d].wait_recv()
@@ -265,7 +263,7 @@
     in_sum = depth % (n * 16) == 0
     chunk = depth // n if in_sum else 16
     span = 2 * reach + 1
-    copies = (1 + rb) * (m - 1) + (1 + rb) * 2 * reach + (2 * (n - 1) if in_sum else 0)
+    copies = 2 * (m - 1) + 4 * reach + (2 * (n - 1) if in_sum else 0)
     vmem = pl.BlockSpec(memory_space=pltpu.VMEM)
     hbm = pl.BlockSpec(memory_space=pltpu.HBM)
     hidden, grad_features, grad_weight = pl.pallas_call(
@@ -287,9 +285,9 @@
             pltpu.VMEM((m * rb * sl + 1, fb, fb), BF16),
             pltpu.VMEM((m * fw, rows), BF16),
             pltpu.VMEM((span * rb, fb, fw), BF16),
-            pltpu.VMEM((rb, 2 * reach, fb, fw), BF16),
-            pltpu.VMEM((rb, 2 * reach, fb, fw), BF16),
-            pltpu.VMEM((rb, m, fb, fw), BF16),
+            pltpu.VMEM((2 * reach, rows, fw), BF16),
+            pltpu.VMEM((2 * reach, rows, fw), BF16),
+            pltpu.VMEM((m, rows, fw), BF16),
             pltpu.VMEM((depth, fw), F32),
             pltpu.VMEM((depth, fw), BF16),
             pltpu.VMEM((n if in_sum else 1, chunk, fw), BF16),

time: 38.4 us -> 38 us (0.990)
  Pallas kernels: 37.6 us -> 37.2 us
where the time goes in v6:
time: 38 us; the launch traced here: 37.9 us
  Pallas kernels  37.2 us (98%)
  between operations  0.64 us (2%)
    pallas_call x1, Pallas kernels, on_device(): pl.pallas_call(functools.partial(kernel, n, m, reach, rb, sl, in_sum), ou...  36.5 us
    pallas_call x1, Pallas kernels, on_device(): pl.pallas_call(store_kernel, out_shape=tuple((jax.ShapeDtypeStruct(v.shap...  0.76 us

profile of v6, /device:TPU:0, one launch (start us, length us, event | category | flops | bytes accessed | tf_op | source)
XLA Modules:
  0.0 37.9 jit_solution(10639255489766009255)
XLA Ops:
  0.6 36.5 %shard_map.85 = (bf16[256,128]{1,0:T(8,128)(2,1)S(1)}, bf16[256,128]{1,0:T(8,128)(2,1)S(1)}, f32[512,128]{1,0:T(8,128)S(1)}) custom-call(s32[2,8]{1,0:T(2,128)} %cols_hbm.1, s32[2]{0:T(128)} %cnt_hbm.1, bf16[256,128]{1,0:T(8,128)(2,1)} %x_hbm.1, bf16[512,128]{1,0:T(8,128)(2,1)} %w_hbm.1, bf16[4,128,128]{2,1,0:T(8,128)(2,1)} %bitcast.1, bf16[256,128]{1,0:T(8,128)(2,1)} %ct_hbm.1), custom_call_target="tpu_custom_call" | custom-call | tf_op jit(solution)/shard_map/pallas_call | solution.py:269
  37.1 0.8 %shard_map.86 = (bf16[256,128]{1,0:T(8,128)(2,1)}, bf16[256,128]{1,0:T(8,128)(2,1)}, f32[512,128]{1,0:T(8,128)}) custom-call(bf16[256,128]{1,0:T(8,128)(2,1)S(1)} %get-tuple-element.6.a, bf16[256,128]{1,0:T(8,128)(2,1)S(1)} %get-tuple-element.7.b, f32[512,128]{1,0:T(8,128)S(1)} %get-tuple-element.8.c), custom_call_target="tpu_custom_call" | custom-call | tf_op jit(solution)/shard_map/pallas_call | solution.py:310

commit v7 on v6

--- a/solution.py
+++ b/solution.py
@@ -155,9 +155,15 @@
     for i in range(m - 2):
         for g in range(rb):
             receive(1 + g, i)
+    loads[2].wait()
+
+    def transpose(first, last):
+        for _, _, _, at, _, _ in place[first * per:last * per]:
+            tl_t[at] = tl[at].T
+
+    transpose(0, m - 1)
     for copy in y_in:
         copy.wait_recv()
-    loads[2].wait()
 
     sums = [jnp.zeros((fb, fw), F32) for _ in range(rb)]
     def add(groups, first, last):
@@ -167,13 +173,12 @@
             blocks = [jnp.where(live, yw[jnp.minimum(where, yw.shape[0] - 1)], jnp.zeros((), BF16))
                       for _, _, _, _, live, where in mine]
             sums[g] = sums[g] + dot(jnp.concatenate(tiles, axis=1), jnp.concatenate(blocks, axis=0), ((1,), (0,)))
-            for tile, (_, _, _, at, _, _) in zip(tiles, mine):
-                tl_t[at] = tile.T
 
     add(range(rb), 0, m - 1)
     for g in range(rb):
         receive(1 + g, m - 2)
         add([g], m - 1, m)
+    transpose(m - 1, m)
     w_in = [push(w_hbm.at[rows_of(lax.rem(f + d, m))], wrow.at[f], "feat", lax.rem(f + d, m)) for d in feat_d]
     pre = jnp.concatenate(sums, axis=0)
     hidden, slope = gelu_and_slope(pre)

time: 38 us -> 37.9 us (level)
  no operation moved by 1% of the time
where the time goes in v7:
time: 37.9 us; the launch traced here: 37.8 us
  Pallas kernels  37.1 us (98%)
  between operations  0.64 us (2%)
    pallas_call x1, Pallas kernels, on_device(): pl.pallas_call(functools.partial(kernel, n, m, reach, rb, sl, in_sum), ou...  36.4 us
    pallas_call x1, Pallas kernels, on_device(): pl.pallas_call(store_kernel, out_shape=tuple((jax.ShapeDtypeStruct(v.shap...  0.76 us

profile of v7, /device:TPU:0, one launch (start us, length us, event | category | flops | bytes accessed | tf_op | source)
XLA Modules:
  0.0 37.8 jit_solution(104600399916929539)
XLA Ops:
  0.6 36.4 %shard_map.85 = (bf16[256,128]{1,0:T(8,128)(2,1)S(1)}, bf16[256,128]{1,0:T(8,128)(2,1)S(1)}, f32[512,128]{1,0:T(8,128)S(1)}) custom-call(s32[2,8]{1,0:T(2,128)} %cols_hbm.1, s32[2]{0:T(128)} %cnt_hbm.1, bf16[256,128]{1,0:T(8,128)(2,1)} %x_hbm.1, bf16[512,128]{1,0:T(8,128)(2,1)} %w_hbm.1, bf16[4,128,128]{2,1,0:T(8,128)(2,1)} %bitcast.1, bf16[256,128]{1,0:T(8,128)(2,1)} %ct_hbm.1), custom_call_target="tpu_custom_call" | custom-call | tf_op jit(solution)/shard_map/pallas_call | solution.py:274
  37.0 0.8 %shard_map.86 = (bf16[256,128]{1,0:T(8,128)(2,1)}, bf16[256,128]{1,0:T(8,128)(2,1)}, f32[512,128]{1,0:T(8,128)}) custom-call(bf16[256,128]{1,0:T(8,128)(2,1)S(1)} %get-tuple-element.6.a, bf16[256,128]{1,0:T(8,128)(2,1)S(1)} %get-tuple-element.7.b, f32[512,128]{1,0:T(8,128)S(1)} %get-tuple-element.8.c), custom_call_target="tpu_custom_call" | custom-call | tf_op jit(solution)/shard_map/pallas_call | solution.py:315

commit v8 on v7

--- a/solution.py
+++ b/solution.py
@@ -109,7 +109,8 @@
         forwards.append((to_right, right))
         forwards.append((to_left, left))
 
-    for kind, src in enumerate([x_hbm] + [t_hbm.at[pl.ds(g * sl, sl)] for g in range(rb)]):
+    own = list(enumerate([x_hbm] + [t_hbm.at[pl.ds(g * sl, sl)] for g in range(rb)]))
+    for kind, src in own[1:2] + own[:1] + own[2:]:
         onward(kind, src, f, 0, f < m - 1, f > 0)
     steps = nearest_first(f, m)
 

time: 37.9 us -> 39.1 us (1.032)
  Pallas kernels: 37.1 us -> 38.3 us
    pallas_call x1, Pallas kernels: 36.4 us -> 37.6 us  [on_device(): pl.pallas_call(functools.partial(kernel, n, m, reach, rb, sl, in_sum), ou...]
where the time goes in v8:
time: 39.1 us; the launch traced here: 39 us
  Pallas kernels  38.3 us (98%)
  between operations  0.64 us (2%)
    pallas_call x1, Pallas kernels, on_device(): pl.pallas_call(functools.partial(kernel, n, m, reach, rb, sl, in_sum), ou...  37.6 us

profile of v8, /device:TPU:0, one launch (start us, length us, event | category | flops | bytes accessed | tf_op | source)
XLA Modules:
  0.0 39.0 jit_solution(4489109948781149080)
XLA Ops:
  0.6 37.6 %shard_map.85 = (bf16[256,128]{1,0:T(8,128)(2,1)S(1)}, bf16[256,128]{1,0:T(8,128)(2,1)S(1)}, f32[512,128]{1,0:T(8,128)S(1)}) custom-call(s32[2,8]{1,0:T(2,128)} %cols_hbm.1, s32[2]{0:T(128)} %cnt_hbm.1, bf16[256,128]{1,0:T(8,128)(2,1)} %x_hbm.1, bf16[512,128]{1,0:T(8,128)(2,1)} %w_hbm.1, bf16[4,128,128]{2,1,0:T(8,128)(2,1)} %bitcast.1, bf16[256,128]{1,0:T(8,128)(2,1)} %ct_hbm.1), custom_call_target="tpu_custom_call" | custom-call | tf_op jit(solution)/shard_map/pallas_call | solution.py:275
  38.2 0.8 %shard_map.86 = (bf16[256,128]{1,0:T(8,128)(2,1)}, bf16[256,128]{1,0:T(8,128)(2,1)}, f32[512,128]{1,0:T(8,128)}) custom-call(bf16[256,128]{1,0:T(8,128)(2,1)S(1)} %get-tuple-element.6.a, bf16[256,128]{1,0:T(8,128)(2,1)S(1)} %get-tuple-element.7.b, f32[512,128]{1,0:T(8,128)S(1)} %get-tuple-element.8.c), custom_call_target="tpu_custom_call" | custom-call | tf_op jit(solution)/shard_map/pallas_call | solution.py:316
